TPU v7x, 32 devices: a whole 2x2x4 slice. The times are simulated.
32 devices in a mesh: blk: 16 (over z, x, core), tp: 2 (over y).
Axes of the slice: x: 2, y: 2, z: 4, core: 2. Of those that a mesh axis runs over, the one named last changes fastest.
Arguments:
- hidden_in: bfloat16 [6144, 4096], P('blk'), may hold values from -6 to 6
- w_query: bfloat16 [4096, 4096], P('blk', 'tp'), may hold values from -0.09375 to 0.09375
- w_key: bfloat16 [4096, 1024], P('blk', 'tp'), may hold values from -0.09375 to 0.09375
- w_value: bfloat16 [4096, 1024], P('blk', 'tp'), may hold values from -0.09375 to 0.09375
- starts: int32 [16], P('blk'), may hold values from 0 to 1152, as said below
- key_cache: bfloat16 [16, 1152, 1024], P('blk', None, 'tp'), may hold values from -400 to 400
- value_cache: bfloat16 [16, 1152, 1024], P('blk', None, 'tp'), may hold values from -6 to 6
- grad_out: bfloat16 [6144, 4096], P('blk', 'tp'), may hold values from -6 to 6
Outputs:
- attended: bfloat16 [6144, 4096], P('blk', 'tp')
- grad_in: bfloat16 [6144, 4096], P('blk', 'tp')
- grad_wq: float32 [4096, 4096], P('blk', 'tp')
- grad_wk: float32 [4096, 1024], P('blk', 'tp')
- grad_wv: float32 [4096, 1024], P('blk', 'tp')
Inputs may be any that keep to these rules, and one draw needn't show every extreme that they name: `starts`: every entry is a multiple of 384; both 0 and 1152 occur.
All inputs are finite; a program needn't handle non-finite values.
Results may differ from a plain program's by a relative error of at most 0.025.
The roundings to bfloat16 on the way count: a program that leaves them out, or rounds other values in their place, can miss the bound.
Values may be sent and summed in bfloat16 or wider, within the bound.
A program may use at most 128 MiB of HBM per device.

v0:
```python
import jax
import jax.numpy as jnp
from jax import lax
from jax.sharding import PartitionSpec as P

H = 32
KV = 8
HD = 128


def contract_last(left, right):
    return lax.dot_general(
        left, right, (((1,), (1,)), ((), ())), preferred_element_type=jnp.float32
    )


def contract_first(left, right):
    return lax.dot_general(
        left, right, (((0,), (0,)), ((), ())), preferred_element_type=jnp.float32
    )


def head_pass(queries, cache_keys, cache_values, fresh_keys, fresh_values, grad_heads, offset):
    groups, row_count, head_width = queries.shape
    cached = cache_keys.shape[0]
    factor = head_width ** (-0.5)
    key_list = jnp.concatenate([cache_keys, fresh_keys], 0)
    value_list = jnp.concatenate([cache_values, fresh_values], 0)
    flat_query = queries.reshape(groups * row_count, head_width)
    flat_grad = grad_heads.reshape(groups * row_count, head_width)
    scores = contract_last(flat_query, key_list) * factor
    scores = scores.reshape(groups, row_count, cached + row_count)
    row_pos = lax.iota(jnp.int32, row_count)
    cache_ok = jnp.broadcast_to(lax.iota(jnp.int32, cached)[None, :] < offset, (row_count, cached))
    own_ok = row_pos[None, :] <= row_pos[:, None]
    allowed = jnp.concatenate([cache_ok, own_ok], 1)
    scores = jnp.where(allowed[None], scores, -jnp.inf)
    row_max = jnp.max(scores, axis=-1, keepdims=True)
    expo = jnp.exp(scores - row_max)
    probs = (expo / jnp.sum(expo, axis=-1, keepdims=True)).astype(jnp.bfloat16)
    probs = probs.reshape(groups * row_count, cached + row_count)
    attended = jnp.dot(probs, value_list, preferred_element_type=jnp.float32).astype(jnp.bfloat16)
    grad_probs = contract_last(flat_grad, value_list)
    probs_wide = probs.astype(jnp.float32)
    row_dot = jnp.sum(probs_wide * grad_probs, axis=-1, keepdims=True)
    grad_scores = (probs_wide * (grad_probs - row_dot) * factor).astype(jnp.bfloat16)
    grad_query = jnp.dot(grad_scores, key_list, preferred_element_type=jnp.float32).astype(
        jnp.bfloat16
    )
    grad_keys = contract_first(grad_scores[:, cached:], flat_query).astype(jnp.bfloat16)
    grad_values = contract_first(probs[:, cached:], flat_grad).astype(jnp.bfloat16)
    return (
        attended.reshape(groups, row_count, head_width),
        grad_query.reshape(groups, row_count, head_width),
        grad_keys,
        grad_values,
    )


def local(hidden_in, w_query, w_key, w_value, starts, key_cache, value_cache, grad_out):
    tokens_dev = hidden_in.shape[0]
    kv_local = w_key.shape[1] // HD
    group = H // KV
    cached = key_cache.shape[1]
    full_query, full_key, full_value = (
        lax.all_gather(w_query, "blk", axis=0, tiled=True),
        lax.all_gather(w_key, "blk", axis=0, tiled=True),
        lax.all_gather(w_value, "blk", axis=0, tiled=True),
    )
    proj_query = jnp.dot(hidden_in, full_query, preferred_element_type=jnp.float32)
    proj_key = jnp.dot(hidden_in, full_key, preferred_element_type=jnp.float32)
    proj_value = jnp.dot(hidden_in, full_value, preferred_element_type=jnp.float32)
    queries = proj_query.astype(jnp.bfloat16)
    new_keys = proj_key.astype(jnp.bfloat16)
    new_values = proj_value.astype(jnp.bfloat16)
    per_query = queries.reshape(tokens_dev, kv_local, group, HD).transpose(1, 2, 0, 3)
    per_grad = grad_out.reshape(tokens_dev, kv_local, group, HD).transpose(1, 2, 0, 3)
    cache_k = key_cache[0].reshape(cached, kv_local, HD).transpose(1, 0, 2)
    cache_v = value_cache[0].reshape(cached, kv_local, HD).transpose(1, 0, 2)
    fresh_k = new_keys.reshape(tokens_dev, kv_local, HD).transpose(1, 0, 2)
    fresh_v = new_values.reshape(tokens_dev, kv_local, HD).transpose(1, 0, 2)
    offset = starts[0]
    results = lax.map(
        lambda packed: head_pass(*packed, offset),
        (per_query, cache_k, cache_v, fresh_k, fresh_v, per_grad),
    )
    attended = results[0].transpose(2, 0, 1, 3).reshape(tokens_dev, kv_local * group * HD)
    grad_query = results[1].transpose(2, 0, 1, 3).reshape(tokens_dev, kv_local * group * HD)
    grad_keys = results[2].transpose(1, 0, 2).reshape(tokens_dev, kv_local * HD)
    grad_values = results[3].transpose(1, 0, 2).reshape(tokens_dev, kv_local * HD)
    input_term = (
        contract_last(grad_query, full_query)
        + contract_last(grad_keys, full_key)
        + contract_last(grad_values, full_value)
    )
    grad_in = lax.psum_scatter(input_term, "tp", scatter_dimension=1, tiled=True).astype(
        jnp.bfloat16
    )
    grads_cat = jnp.concatenate([grad_query, grad_keys, grad_values], 1)
    blk_count = lax.axis_size("blk")
    summed = lax.psum_scatter(
        contract_first(hidden_in, grads_cat), "blk", scatter_dimension=0, tiled=True
    )
    summed = summed * (tokens_dev * blk_count) ** (-0.5)
    query_cols = w_query.shape[1]
    kv_cols = w_key.shape[1]
    grad_wq = summed[:, :query_cols]
    grad_wk = summed[:, query_cols : query_cols + kv_cols]
    grad_wv = summed[:, query_cols + kv_cols :]
    return (attended, grad_in, grad_wq, grad_wk, grad_wv)


def solution(mesh):
    in_specs = (
        P("blk", None),
        P("blk", "tp"),
        P("blk", "tp"),
        P("blk", "tp"),
        P("blk"),
        P("blk", None, "tp"),
        P("blk", None, "tp"),
        P("blk", "tp"),
    )
    out_specs = (P("blk", "tp"), P("blk", "tp"), P("blk", "tp"), P("blk", "tp"), P("blk", "tp"))
    return jax.shard_map(local, mesh=mesh, in_specs=in_specs, out_specs=out_specs, check_vma=False)
```

profile of v0, /device:TPU:0, one launch (start us, length us, event | category | flops | bytes accessed | tf_op | source)
XLA Modules:
  0.0 1083.7 jit_solution(5784492922681254008)
XLA Ops:
  16.8 46.6 %all-gather.8.cloned.1.call-done = bf16[4096,512]{1,0:T(8,128)(2,1)} async-done(((bf16[256,512]{1,0:T(8,128)(2,1)}), bf16[4096,512]{1,0:T(8,128)(2,1)}) %all-gather.8.cloned.1.call-update) | async-done | bytes 4194320 | tf_op jit(solution)/shard_map/all_gather | solution.py:68
  63.5 4.0 fusion.32
  68.3 46.4 %all-gather.6.cloned.1.call-done = bf16[4096,512]{1,0:T(8,128)(2,1)} async-done(((bf16[256,512]{1,0:T(8,128)(2,1)}), bf16[4096,512]{1,0:T(8,128)(2,1)}) %all-gather.6.cloned.1.call-update) | async-done | bytes 4194320 | tf_op jit(solution)/shard_map/all_gather | solution.py:67
  114.7 4.0 fusion.31
  119.5 122.8 %all-gather.4.cloned.1.call-done = bf16[4096,2048]{1,0:T(8,128)(2,1)} async-done(((bf16[256,2048]{1,0:T(8,128)(2,1)}), bf16[4096,2048]{1,0:T(8,128)(2,1)}) %all-gather.4.cloned.1.call-update) | async-done | bytes 16777232 | tf_op jit(solution)/shard_map/all_gather | solution.py:66
  242.3 11.6 %convolution_convert_fusion.2 = bf16[384,2048]{1,0:T(8,128)(2,1)} fusion(bf16[384,4096]{1,0:T(8,128)(2,1)S(1)} %copy-done, bf16[4096,2048]{1,0:T(8,128)(2,1)} %all-gather.4.cloned.1.call-done), kind=kOutput, calls=%fused_computation.42 | convolution fusion | flops 6443237376 | bytes 21495808 | tf_op jit(solution)/shard_map/dot_general | solution.py:70
  253.9 3.8 reshape.70
  260.6 237.0 %while.16 = (s32[]{:T(128)}, bf16[4,4,384,128]{3,2,1,0:T(8,128)(2,1)}, bf16[4,4,384,128]{2,3,1,0:T(8,128)(2,1)}, bf16[4,384,128]{1,2,0:T(8,128)(2,1)}, bf16[4,38...) while((s32[]{:T(128)}, ...), condition=%wide.region_4.5_spmd, body=%wide.region_0.4_spmd.sunk | while | flops 2760028672 | bytes 159401600 | solution.py:83
  279.8 9.6 fusion.81
  289.3 9.6 fusion.82
  299.0 4.5 convolution_convert_fusion.8
  311.2 3.8 convolution_convert_fusion.7
  339.0 9.6 fusion.81
  348.6 9.6 fusion.82
  358.2 4.5 convolution_convert_fusion.8
  370.5 3.8 convolution_convert_fusion.7
  398.3 9.6 fusion.81
  407.8 9.6 fusion.82
  417.5 4.5 convolution_convert_fusion.8
  429.7 3.8 convolution_convert_fusion.7
  457.5 9.6 fusion.81
  467.1 9.6 fusion.82
  476.7 4.5 convolution_convert_fusion.8
  489.0 3.8 convolution_convert_fusion.7
  497.6 10.8 fusion.36
  508.5 4.2 fusion.37
  512.7 4.8 add_add_fusion
  517.5 21.5 %convolution_bitcast_fusion = f32[4096,3072]{0,1:T(8,128)} fusion(bf16[384,4096]{1,0:T(8,128)(2,1)S(1)} %copy-done, bf16[384,512]{0,1:T(8,128)(2,1)} %bitcast.132, bf16[384,512]{0,1:T(8,128)(2,1)S(1)} %bitcast.131, bf16[384,2048]{0,1:T(8,128)(2,1)} %bitcast.136), kind=kOutput, calls=%fused_computation.40 | convolution fusion | flops 9670754304 | bytes 55836672 | tf_op jit(solution)/shard_map/dot_general | solution.py:18
  539.1 3.8 copy.29
  542.9 3.8 reshape.74
  546.7 46.2 %reduce-scatter.3.cloned.1.call-done = f32[384,2048]{1,0:T(8,128)} async-done(((f32[384,4096]{1,0:T(8,128)}), f32[384,2048]{1,0:T(8,128)}) %reduce-scatter.3.cloned.1.call-update) | async-done | bytes 3145744 | tf_op jit(solution)/shard_map/reduce_scatter | solution.py:96
  596.1 469.4 %reduce-scatter.5.cloned.1.call-done = f32[256,3072]{0,1:T(8,128)} async-done(((f32[4096,3072]{0,1:T(8,128)}), f32[256,3072]{0,1:T(8,128)}) %reduce-scatter.5.cloned.1.call-update) | async-done | bytes 3145744 | tf_op jit(solution)/shard_map/reduce_scatter | solution.py:101
  (195 shorter events, 155.2 us)
Async XLA Ops:
  7.2 56.3 %copy-start = (bf16[384,4096]{1,0:T(8,128)(2,1)S(1)}, bf16[384,4096]{1,0:T(8,128)(2,1)}, u32[]{:S(2)}) copy-start(bf16[384,4096]{1,0:T(8,128)(2,1)} %param.10) | copy-start | bytes 9437188
  7.2 56.3 %all-gather.8.cloned.1.call-start = ((), (), s32[]{:S(2)}) async-start(), calls=%async_computation.4 | async-start | bytes 4456448 | tf_op jit(solution)/shard_map/all_gather | solution.py:68
  7.9 106.8 %all-gather.6.cloned.1.call-start = ((), (), s32[]{:S(2)}) async-start(), calls=%async_computation.3 | async-start | bytes 4456448 | tf_op jit(solution)/shard_map/all_gather | solution.py:67
  8.7 233.6 %all-gather.4.cloned.1.call-start = ((), (), s32[]{:S(2)}) async-start(), calls=%async_computation.2 | async-start | bytes 17825792 | tf_op jit(solution)/shard_map/all_gather | solution.py:66
  9.4 583.5 %reduce-scatter.3.cloned.1.call-start = ((), (), s32[]{:S(2)}) async-start(), calls=%async_computation.5 | async-start | bytes 9437184 | tf_op jit(solution)/shard_map/reduce_scatter | solution.py:96
  265.9 5.5 copy-start.8
  267.0 4.5 copy-start.4
  289.3 9.6 copy-start.2
  289.3 9.6 copy-start.6
  289.3 9.6 copy-start.9
  305.5 10.3 copy-start.3
  325.2 5.5 copy-start.8
  326.2 4.5 copy-start.4
  348.6 9.6 copy-start.2
  348.6 9.6 copy-start.6
  348.6 9.6 copy-start.9
  364.8 10.3 copy-start.3
  384.4 5.5 copy-start.8
  385.5 4.5 copy-start.4
  407.8 9.6 copy-start.2
  407.8 9.6 copy-start.6
  407.8 9.6 copy-start.9
  424.0 10.3 copy-start.3
  443.7 5.5 copy-start.8
  444.7 4.5 copy-start.4
  467.1 9.6 copy-start.2
  467.1 9.6 copy-start.6
  467.1 9.6 copy-start.9
  483.3 10.3 copy-start.3
  497.6 10.8 copy-start.10
  508.5 4.2 copy-start.7
  517.5 548.1 %reduce-scatter.5.cloned.1.call-start = ((), (), s32[]{:S(2)}) async-start(), calls=%async_computation.6 | async-start | bytes 53477376 | tf_op jit(solution)/shard_map/reduce_scatter | solution.py:101
  (9 other events, 33.7 us)
Sparse Core Ops, SparseCore 0:
  10.2 53.2 all-gather.7
  65.6 49.0 all-gather.5
  116.9 125.3 all-gather.3
  517.6 75.2 reduce-scatter.2
  597.6 467.9 reduce-scatter.4
where the time goes:
time: 1090 us; the launch traced here: 1080 us
  waiting for transfers between devices  734 us (67%)
  matrix products  159 us (15%)
  local copies, waits for them, and re-layouts  123 us (11%)
  other arithmetic  53.3 us (5%)
  between operations  13.9 us (1%)
    reduce_scatter x1, waiting for transfers between devices, local(): lax.psum_scatter(contract_first(hidden_in, grads_cat), 'blk', scatter_dim...  469 us
    all_gather x1, waiting for transfers between devices, local(): lax.all_gather(w_query, 'blk', axis=0, tiled=True)  123 us
    dot_general x11, matrix products, contract_last(): lax.dot_general(left, right, (((1,), (1,)), ((), ())), preferred_element_...  65 us
    all_gather x1, waiting for transfers between devices, local(): lax.all_gather(w_value, 'blk', axis=0, tiled=True)  46.6 us
    all_gather x1, waiting for transfers between devices, local(): lax.all_gather(w_key, 'blk', axis=0, tiled=True)  46.4 us
    reduce_scatter x1, waiting for transfers between devices, local(): lax.psum_scatter(input_term, 'tp', scatter_dimension=1, tiled=True)  46.2 us
    dot_general x9, matrix products, contract_first(): lax.dot_general(left, right, (((0,), (0,)), ((), ())), preferred_element_...  41 us
    convert_element_type x4, other arithmetic, head_pass(): (probs_wide * (grad_probs - row_dot) * factor).astype(jnp.bfloat16)  38.5 us
  transfers between devices with their start and end apart: 5, of which 5 were waited for; matrix products, arithmetic and copies ran while one was open for 5% of the time, Pallas kernels for 0%

commit v1 on v0

v1 whole, which is shorter than its diff:
```python
import functools

import jax
import jax.numpy as jnp
from jax import lax
from jax.experimental import pallas as pl
from jax.experimental.pallas import tpu as pltpu
from jax.sharding import PartitionSpec as P

H = 32
KV = 8
HD = 128
MESH = pl.DeviceIdType.MESH
LOG2E = 1.4426950408889634
VMEM_LIMIT = 60 * 1024 * 1024


def contract_last(left, right):
    return lax.dot_general(
        left, right, (((1,), (1,)), ((), ())), preferred_element_type=jnp.float32
    )


def contract_first(left, right):
    return lax.dot_general(
        left, right, (((0,), (0,)), ((), ())), preferred_element_type=jnp.float32
    )


def ring_position(chip, n):
    half = n // 2
    if n == 8:
        z, x = chip // 2, chip % 2
    else:
        z, x = chip % half, chip // half
    return z + x * (n - 1 - 2 * z)


def ring_chip(position, n):
    half = n // 2
    x = position // half
    z = position + x * (n - 1 - 2 * position)
    return z * 2 + x if n == 8 else x * half + z


def places(n):
    blk = lax.axis_index("blk")
    core, chip = blk % 2, blk // 2
    position = ring_position(chip, n)

    def device(pos):
        return ring_chip((pos + 2 * n) % n, n) * 2 + core

    return blk, chip * 2 + 1 - core, position, device


def gather_kernel(
    n, w_ref, hidden_ref, full_ref, pair_ref,
    own_sem, own_send, own_recv, hid_send, hid_recv, ring_send, ring_recv, fwd_send, fwd_recv,
):
    blk, sibling, position, device = places(n)
    target = (device(position + 1), device(position - 1))
    quarter = w_ref.shape[0] // 4
    barrier = pltpu.get_barrier_semaphore()
    for other in (sibling,) + target:
        pl.semaphore_signal(barrier, inc=1, device_id={"blk": other}, device_id_type=MESH)
    pl.semaphore_wait(barrier, 3)

    def origin(way, step):
        return device(position - step) if way == 0 else device(position + step)

    def rows(way, k):
        return pl.ds((way * 2 + k) * quarter, quarter)

    def ring_copy(way, k, step, src, index):
        return pltpu.make_async_remote_copy(
            src_ref=src,
            dst_ref=full_ref.at[index, rows(way, k)],
            send_sem=ring_send.at[way, k, step],
            recv_sem=ring_recv.at[way, k, step],
            device_id={"blk": target[way]},
            device_id_type=MESH,
        )

    def forward(way, k, step, index):
        return pltpu.make_async_remote_copy(
            src_ref=full_ref.at[index, rows(way, k)],
            dst_ref=full_ref.at[index, rows(way, k)],
            send_sem=fwd_send.at[way, k, step],
            recv_sem=fwd_recv.at[way, k, step],
            device_id={"blk": sibling},
            device_id_type=MESH,
        )

    for k in range(2):
        for way in range(2):
            ring_copy(way, k, 0, w_ref.at[rows(way, k)], blk).start()
    own = pltpu.make_async_copy(w_ref, full_ref.at[blk], own_sem)
    own.start()
    share = pltpu.make_async_remote_copy(
        src_ref=w_ref, dst_ref=full_ref.at[blk], send_sem=own_send, recv_sem=own_recv,
        device_id={"blk": sibling}, device_id_type=MESH,
    )
    share.start()
    share_hidden = pltpu.make_async_remote_copy(
        src_ref=hidden_ref, dst_ref=pair_ref, send_sem=hid_send, recv_sem=hid_recv,
        device_id={"blk": sibling}, device_id_type=MESH,
    )
    share_hidden.start()

    def step_body(step, carry):
        for k in range(2):
            for way in range(2):
                index = origin(way, step)
                here = full_ref.at[index, rows(way, k)]
                ring_copy(way, k, step - 1, here, index).wait_recv()

                @pl.when(step < n - 1)
                def _():
                    ring_copy(way, k, step, here, index).start()

                forward(way, k, step - 1, index).start()
        return carry

    lax.fori_loop(1, n, step_body, 0)

    def drain(step, carry):
        for k in range(2):
            for way in range(2):
                index = origin(way, step)
                here = full_ref.at[index, rows(way, k)]
                ring_copy(way, k, step, here, index).wait_send()
                far = origin(way, step + 1)
                mate = far + sibling - blk
                forward(way, k, step, far).wait_send()
                forward(way, k, step, mate).wait_recv()
        return carry

    lax.fori_loop(0, n - 1, drain, 0)
    own.wait()
    share.wait_send()
    pltpu.make_async_remote_copy(
        src_ref=w_ref, dst_ref=full_ref.at[sibling], send_sem=own_send, recv_sem=own_recv,
        device_id={"blk": sibling}, device_id_type=MESH,
    ).wait_recv()
    share_hidden.wait()


def gather(w, hidden, blk_count):
    n = blk_count // 2
    rows, cols = w.shape
    dma = pltpu.SemaphoreType.DMA
    return pl.pallas_call(
        functools.partial(gather_kernel, n),
        out_shape=(
            jax.ShapeDtypeStruct((blk_count, rows, cols), w.dtype),
            jax.ShapeDtypeStruct(hidden.shape, hidden.dtype),
        ),
        in_specs=[pl.BlockSpec(memory_space=pl.ANY)] * 2,
        out_specs=[pl.BlockSpec(memory_space=pl.ANY)] * 2,
        scratch_shapes=[dma, dma, dma, dma, dma] + [dma((2, 2, n - 1))] * 4,
        compiler_params=pltpu.CompilerParams(collective_id=0, has_side_effects=True),
        name="ring_gather",
    )(w, hidden)


def scatter_kernel(
    n, tp_count, scale, hid_ref, mate_ref, grads_ref, term_ref, out_ref, recv_term_ref,
    mate_grads, part, send_buf, recv_buf,
    gr_send, gr_recv, term_send, term_recv, ring_send, ring_recv,
):
    blk, sibling, position, device = places(n)
    target = (device(position + 1), device(position - 1))
    tp_me = lax.axis_index("tp")
    height, width = out_ref.shape
    half_rows, half = height // 2, width // 2
    tile = 384 if half % 384 == 0 else 128
    chunk = term_ref.shape[1] // tp_count
    barrier = pltpu.get_barrier_semaphore()
    for other in (sibling,) + target:
        pl.semaphore_signal(barrier, inc=1, device_id={"blk": other}, device_id_type=MESH)
    for k in range(1, tp_count):
        pl.semaphore_signal(
            barrier, inc=1, device_id={"tp": (tp_me + k) % tp_count}, device_id_type=MESH
        )
    pl.semaphore_wait(barrier, 3 + tp_count - 1)

    share = pltpu.make_async_remote_copy(
        src_ref=grads_ref, dst_ref=mate_grads, send_sem=gr_send, recv_sem=gr_recv,
        device_id={"blk": sibling}, device_id_type=MESH,
    )
    share.start()
    terms = []
    for k in range(1, tp_count):
        peer = (tp_me + k) % tp_count
        copy = pltpu.make_async_remote_copy(
            src_ref=term_ref.at[:, pl.ds(pl.multiple_of(peer * chunk, 128), chunk)],
            dst_ref=recv_term_ref.at[k - 1],
            send_sem=term_send.at[k - 1],
            recv_sem=term_recv.at[k - 1],
            device_id={"tp": peer},
            device_id_type=MESH,
        )
        copy.start()
        terms.append(copy)
    share.wait()

    def ring_copy(way, k, step):
        spot = pl.ds(k * half_rows, half_rows)
        return pltpu.make_async_remote_copy(
            src_ref=send_buf.at[way, step, spot],
            dst_ref=recv_buf.at[way, step, spot],
            send_sem=ring_send.at[way, k, step],
            recv_sem=ring_recv.at[way, k, step],
            device_id={"blk": target[way]},
            device_id_type=MESH,
        )

    def step_body(step, carry):
        for way in range(2):
            owner = device(position - 1 - step) if way == 0 else device(position + 1 + step)
            columns = pl.ds(pl.multiple_of(owner * height, 128), height)

            def tile_body(t, inner):
                at = pl.multiple_of(way * half + t * tile, 128)
                to = pl.multiple_of(t * tile, 128)
                part[way, :, pl.ds(to, tile)] = contract_first(
                    hid_ref[:, columns], grads_ref[:, pl.ds(at, tile)]
                ) + contract_first(mate_ref[:, columns], mate_grads[:, pl.ds(at, tile)])
                return inner

            lax.fori_loop(0, half // tile, tile_body, 0)
        for k in range(2):
            for way in range(2):
                spot = pl.ds(k * half_rows, half_rows)

                @pl.when(step > 0)
                def _():
                    before = step - 1
                    ring_copy(way, k, before).wait_recv()
                    part[way, spot] += recv_buf[way, before, spot].astype(jnp.float32)

                @pl.when(step < n - 1)
                def _():
                    send_buf[way, step, spot] = part[way, spot].astype(jnp.bfloat16)
                    ring_copy(way, k, step).start()

        return carry

    lax.fori_loop(0, n, step_body, 0)
    for way in range(2):
        out_ref[:, way * half : (way + 1) * half] = part[way] * scale

    def drain(step, carry):
        for k in range(2):
            for way in range(2):
                ring_copy(way, k, step).wait_send()
        return carry

    lax.fori_loop(0, n - 1, drain, 0)
    for copy in terms:
        copy.wait()


def scatter(hidden, mate, grads, term, blk_count, tp_count, scale):
    n = blk_count // 2
    tokens, depth = hidden.shape
    height, width = depth // blk_count, grads.shape[1]
    half = width // 2
    dma = pltpu.SemaphoreType.DMA
    vmem = pl.BlockSpec(memory_space=pltpu.VMEM)
    hbm = pl.BlockSpec(memory_space=pl.ANY)
    return pl.pallas_call(
        functools.partial(scatter_kernel, n, tp_count, scale),
        out_shape=(
            jax.ShapeDtypeStruct((height, width), jnp.float32),
            jax.ShapeDtypeStruct((tp_count - 1, tokens, depth // tp_count), jnp.bfloat16),
        ),
        in_specs=[vmem, vmem, vmem, hbm],
        out_specs=[vmem, hbm],
        scratch_shapes=[
            pltpu.VMEM((tokens, width), jnp.bfloat16),
            pltpu.VMEM((2, height, half), jnp.float32),
            pltpu.VMEM((2, n - 1, height, half), jnp.bfloat16),
            pltpu.VMEM((2, n - 1, height, half), jnp.bfloat16),
            dma,
            dma,
            dma((tp_count - 1,)),
            dma((tp_count - 1,)),
            dma((2, 2, n - 1)),
            dma((2, 2, n - 1)),
        ],
        compiler_params=pltpu.CompilerParams(
            collective_id=1, has_side_effects=True, vmem_limit_bytes=VMEM_LIMIT
        ),
        name="ring_scatter",
    )(hidden, mate, grads, term)


def attention_kernel(
    starts_ref, q_ref, kn_ref, vn_ref, kc_ref, vc_ref, go_ref,
    att_ref, gq_ref, gk_ref, gv_ref, gk_acc, gv_acc,
):
    member, group = pl.program_id(1), pl.num_programs(1)
    rows, cached = q_ref.shape[0], kc_ref.shape[1]
    factor = HD ** (-0.5)
    q, go = q_ref[...], go_ref[...]
    kn, vn, kc, vc = kn_ref[...], vn_ref[...], kc_ref[0], vc_ref[0]
    slot = lax.broadcasted_iota(jnp.int32, (rows, cached), 1)
    s_c = jnp.where(slot < starts_ref[0], contract_last(q, kc), -jnp.inf)
    row = lax.broadcasted_iota(jnp.int32, (rows, rows), 0)
    col = lax.broadcasted_iota(jnp.int32, (rows, rows), 1)
    s_o = jnp.where(col <= row, contract_last(q, kn), -jnp.inf)
    top = jnp.maximum(
        jnp.max(s_c, axis=-1, keepdims=True), jnp.max(s_o, axis=-1, keepdims=True)
    )
    e_c = jnp.exp2((s_c - top) * (factor * LOG2E))
    e_o = jnp.exp2((s_o - top) * (factor * LOG2E))
    total = jnp.sum(e_c, axis=-1, keepdims=True) + jnp.sum(e_o, axis=-1, keepdims=True)
    inverse = 1.0 / total
    p_c = (e_c * inverse).astype(jnp.bfloat16)
    p_o = (e_o * inverse).astype(jnp.bfloat16)
    att = jnp.dot(p_c, vc, preferred_element_type=jnp.float32) + jnp.dot(
        p_o, vn, preferred_element_type=jnp.float32
    )
    att_ref[...] = att.astype(jnp.bfloat16)
    row_dot = jnp.sum(att * go.astype(jnp.float32), axis=-1, keepdims=True)
    g_c = contract_last(go, vc) - row_dot
    g_o = contract_last(go, vn) - row_dot
    ds_c = (p_c.astype(jnp.float32) * g_c * factor).astype(jnp.bfloat16)
    ds_o = (p_o.astype(jnp.float32) * g_o * factor).astype(jnp.bfloat16)
    gq = jnp.dot(ds_c, kc, preferred_element_type=jnp.float32) + jnp.dot(
        ds_o, kn, preferred_element_type=jnp.float32
    )
    gq_ref[...] = gq.astype(jnp.bfloat16)

    @pl.when(member == 0)
    def _():
        gk_acc[...] = jnp.zeros_like(gk_acc)
        gv_acc[...] = jnp.zeros_like(gv_acc)

    gk_acc[...] += contract_first(ds_o, q)
    gv_acc[...] += contract_first(p_o, go)

    @pl.when(member == group - 1)
    def _():
        gk_ref[...] = gk_acc[...].astype(jnp.bfloat16)
        gv_ref[...] = gv_acc[...].astype(jnp.bfloat16)


def attention(starts, proj, key_cache, value_cache, grad_out):
    tokens = proj.shape[0]
    kv_local = key_cache.shape[2] // HD
    cached = key_cache.shape[1]
    group = H // KV
    heads = kv_local * group
    per_head = pl.BlockSpec((tokens, HD), lambda g, m: (0, g * group + m))
    per_kv = pl.BlockSpec((tokens, HD), lambda g, m: (0, g))
    cache = pl.BlockSpec((1, cached, HD), lambda g, m: (0, 0, g))
    bf16 = jnp.bfloat16
    return pl.pallas_call(
        attention_kernel,
        grid=(kv_local, group),
        out_shape=(
            jax.ShapeDtypeStruct((tokens, heads * HD), bf16),
            jax.ShapeDtypeStruct((tokens, heads * HD), bf16),
            jax.ShapeDtypeStruct((tokens, kv_local * HD), bf16),
            jax.ShapeDtypeStruct((tokens, kv_local * HD), bf16),
        ),
        in_specs=[
            pl.BlockSpec(memory_space=pltpu.SMEM),
            per_head,
            pl.BlockSpec((tokens, HD), lambda g, m: (0, heads + g)),
            pl.BlockSpec((tokens, HD), lambda g, m: (0, heads + kv_local + g)),
            cache,
            cache,
            per_head,
        ],
        out_specs=[per_head, per_head, per_kv, per_kv],
        scratch_shapes=[pltpu.VMEM((tokens, HD), jnp.float32)] * 2,
        compiler_params=pltpu.CompilerParams(vmem_limit_bytes=VMEM_LIMIT),
        name="attention",
    )(starts, proj, proj, proj, key_cache, value_cache, grad_out)


def local(blk_count, tp_count, hidden_in, w_query, w_key, w_value, starts, key_cache, value_cache, grad_out):
    tokens_dev, depth = hidden_in.shape
    w = jnp.concatenate([w_query, w_key, w_value], 1)
    full, mate = gather(w, hidden_in, blk_count)
    full = full.reshape(depth, w.shape[1])
    proj = jnp.dot(hidden_in, full, preferred_element_type=jnp.float32).astype(jnp.bfloat16)
    attended, grad_query, grad_keys, grad_values = attention(
        starts, proj, key_cache, value_cache, grad_out
    )
    grads = jnp.concatenate([grad_query, grad_keys, grad_values], 1)
    term = contract_last(grads, full)
    scale = (tokens_dev * blk_count) ** (-0.5)
    summed, others = scatter(
        hidden_in, mate, grads, term.astype(jnp.bfloat16), blk_count, tp_count, scale
    )
    width = depth // tp_count
    grad_in = lax.dynamic_slice_in_dim(term, lax.axis_index("tp") * width, width, 1)
    for k in range(tp_count - 1):
        grad_in = grad_in + others[k].astype(jnp.float32)
    grad_in = grad_in.astype(jnp.bfloat16)
    query_cols, kv_cols = w_query.shape[1], w_key.shape[1]
    return (
        attended,
        grad_in,
        summed[:, :query_cols],
        summed[:, query_cols : query_cols + kv_cols],
        summed[:, query_cols + kv_cols :],
    )


def solution(mesh):
    in_specs = (
        P("blk", None),
        P("blk", "tp"),
        P("blk", "tp"),
        P("blk", "tp"),
        P("blk"),
        P("blk", None, "tp"),
        P("blk", None, "tp"),
        P("blk", "tp"),
    )
    out_specs = (P("blk", "tp"),) * 5
    return jax.shard_map(
        functools.partial(local, mesh.shape["blk"], mesh.shape["tp"]),
        mesh=mesh,
        in_specs=in_specs,
        out_specs=out_specs,
        check_vma=False,
    )
```

time: 1090 us -> 355 us (0.33)
  waiting for transfers between devices: 734 us -> 0 us
  Pallas kernels: 0 us -> 310 us
  matrix products: 159 us -> 33 us
  local copies, waits for them, and re-layouts: 123 us -> 4.29 us
  other arithmetic: 53.3 us -> 6.86 us
  between operations: 13.9 us -> 1.37 us
    reduce_scatter x2 -> x0, waiting for transfers between devices: 516 us -> none  [the longest x1 469 us: local(): lax.psum_scatter(contract_first(hidden_in, grads_cat), 'blk', scatter_dim...]
    pallas_call x0 -> x3, Pallas kernels: none -> 310 us  [the longest x1 136 us: scatter(): pl.pallas_call(functools.partial(scatter_kernel, n, tp_count, scale), out...]
    all_gather x3 -> x0, waiting for transfers between devices: 216 us -> none  [the longest x1 123 us: local(): lax.all_gather(w_query, 'blk', axis=0, tiled=True)]
    dot_general x20 -> x1, matrix products: 94 us -> 15.3 us  [local(): jnp.dot(hidden_in, full, preferred_element_type=jnp.float32)]
    dot_general x11 -> x1, matrix products: 65 us -> 17.7 us  [contract_last(): lax.dot_general(left, right, (((1,), (1,)), ((), ())), preferred_element_...]
    convert_element_type x5 -> x1, other arithmetic: 41.8 us -> 4.18 us  [local(): grad_in = grad_in.astype(jnp.bfloat16)]
    dynamic_update_slice x28 -> x0, local copies, waits for them, and re-layouts: 30.5 us -> none  [local(): lax.map(lambda packed: head_pass(*packed, offset), (per_query, cache_k, c...]
    dynamic_slice x24 -> x0, local copies, waits for them, and re-layouts: 30.5 us -> none  [local(): lax.map(lambda packed: head_pass(*packed, offset), (per_query, cache_k, c...]
  transfers between devices with their start and end apart: 5 -> 0, of which waited for: 5 -> 0; matrix products, arithmetic and copies ran while one was open for 5% -> 0% of each run, Pallas kernels for 0% -> 0%
where the time goes in v1:
time: 355 us
  Pallas kernels  310 us (87%)
  matrix products  33 us (9%)
  other arithmetic  6.86 us (2%)
  local copies, waits for them, and re-layouts  4.29 us (1%)
    pallas_call x1, Pallas kernels, scatter(): pl.pallas_call(functools.partial(scatter_kernel, n, tp_count, scale), out...  136 us
    pallas_call x1, Pallas kernels, gather(): pl.pallas_call(functools.partial(gather_kernel, n), out_shape=(jax.ShapeD...  127 us
    pallas_call x1, Pallas kernels, attention(): pl.pallas_call(attention_kernel, grid=(kv_local, group), out_shape=(jax.S...  46.7 us
    dot_general x1, matrix products, contract_last(): lax.dot_general(left, right, (((1,), (1,)), ((), ())), preferred_element_...  17.7 us
    dot_general x1, matrix products, local(): jnp.dot(hidden_in, full, preferred_element_type=jnp.float32)  15.3 us

profile of v1, /device:TPU:0, one launch (start us, length us, event | category | flops | bytes accessed | tf_op | source)
XLA Modules:
  0.0 355.0 jit_solution(11431176776345680589)
XLA Ops:
  1.3 2.7 pad_maximum_fusion.w_ref
  4.0 0.0 copy-start
  4.0 126.5 %ring_gather.1 = (bf16[16,256,3072]{2,1,0:T(8,128)(2,1)}, bf16[384,4096]{1,0:T(8,128)(2,1)}) custom-call(bf16[256,3072]{1,0:T(8,128)(2,1)} %pad_maximum_fusion.w_ref, bf16[384,4096]{1,0:T(8,128)(2,1)} %hid_ref.1), custom_call_target="tpu_custom_call" | custom-call | tf_op jit(solution)/shard_map/ring_gather/pallas_call | solution.py:153
  130.5 0.0 copy-done
  130.5 15.3 %fusion.q_ref.kn_ref.vn_ref = bf16[384,3072]{1,0:T(8,128)(2,1)} fusion(bf16[384,4096]{1,0:T(8,128)(2,1)S(1)} %copy-done, bf16[4096,3072]{1,0:T(8,128)(2,1)} %bitcast.10), kind=kOutput, calls=%fused_computation.1 | convolution fusion | flops 9664856064 | bytes 30670848 | tf_op jit(solution)/shard_map/dot_general | solution.py:391
  145.8 46.7 %attention.1 = (bf16[384,2048]{1,0:T(8,128)(2,1)}, bf16[384,2048]{1,0:T(8,128)(2,1)}, bf16[384,512]{1,0:T(8,128)(2,1)}, bf16[384,512]{1,0:T(8,128)(2,1)}) custom-call(s32[1]{0:T(128)S(6)} %copy.17.starts_ref, bf16[384,3072]{1,0:T(8,128)(2,1)} %fusion.q_ref.kn_ref.vn_ref, bf16[384,3072]{1,0:T(8,128)(2,1)} %fusion.q_ref.kn_ref.vn_ref, ...), custom_call_target="tpu_custom_call" | custom-call | tf_op jit(solution)/shard_map/attention/pallas_call | solution.py:361
  192.4 0.0 copy-start.4
  192.4 0.0 copy-start.3
  192.5 1.6 constant_dynamic-update-slice_fusion.2
  194.1 0.0 copy-done.4
  194.1 0.0 copy-done.3
  194.2 0.0 copy-start.1
  194.2 17.7 %fusion.3 = (bf16[384,4096]{1,0:T(8,128)(2,1)}, f32[384,4096]{1,0:T(8,128)}) fusion(bf16[384,3072]{1,0:T(8,128)(2,1)S(1)} %constant_dynamic-update-slice_fusion.grads_ref, bf16[4096,3072]{1,0:T(8,128)(2,1)} %bitcast.11), kind=kOutput, calls=%fused_computation.9 | convolution fusion | flops 9665249280 | bytes 36962304 | tf_op jit(solution)/shard_map/dot_general | solution.py:19
  211.9 0.0 copy-done.1
  211.9 136.3 %ring_scatter.1 = (f32[256,3072]{1,0:T(8,128)}, bf16[1,384,2048]{2,1,0:T(8,128)(2,1)}) custom-call(bf16[384,4096]{1,0:T(8,128)(2,1)} %hid_ref.1, bf16[384,4096]{1,0:T(8,128)(2,1)} %get-tuple-element.18.mate_ref, bf16[384,3072]{1,0:T(8,128)(2,1)} %copy-done.1, bf16[384,4096]{1,0:T(8,128)(2,1)} %get-tuple-element.23.term_ref), custom_call_target="tpu_custom_call" | custom-call | tf_op jit(solution)/shard_map/ring_scatter/pallas_call | solution.py:273
  348.2 0.0 copy-start.2
  348.3 4.2 %fusion.1 = bf16[384,2048]{1,0:T(8,128)(2,1)} fusion(f32[384,4096]{1,0:T(8,128)} %get-tuple-element.24, s32[]{:T(128)S(6)} %select_n.3, bf16[1,384,2048]{2,1,0:T(8,128)(2,1)} %get-tuple-element.19), kind=kLoop, calls=%fused_computation.3 | loop fusion | flops 2359296 | bytes 6291460 | tf_op jit(solution)/shard_map/convert_element_type | solution.py:405
  352.4 0.0 copy-done.2
  352.4 1.5 slice.9
  354.0 1.0 fusion.2
  (2 shorter events, 0.1 us)
Async XLA Ops:
  4.0 126.5 %copy-start = (bf16[384,4096]{1,0:T(8,128)(2,1)S(1)}, bf16[384,4096]{1,0:T(8,128)(2,1)}, u32[]{:S(2)}) copy-start(bf16[384,4096]{1,0:T(8,128)(2,1)} %hid_ref.1) | copy-start | bytes 9437188
  192.4 1.6 copy-start.4
  192.4 1.7 copy-start.3
  194.2 17.7 %copy-start.1 = (bf16[384,3072]{1,0:T(8,128)(2,1)}, bf16[384,3072]{1,0:T(8,128)(2,1)S(1)}, u32[]{:S(2)}) copy-start(bf16[384,3072]{1,0:T(8,128)(2,1)S(1)} %constant_dynamic-update-slice_fusion.grads_ref) | copy-start | bytes 7077892
  348.2 4.2 %copy-start.2 = (f32[256,3072]{1,0:T(8,128)S(1)}, f32[256,3072]{1,0:T(8,128)}, u32[]{:S(2)}) copy-start(f32[256,3072]{1,0:T(8,128)} %get-tuple-element.20) | copy-start | bytes 9437188

commit v2 on v1

--- a/solution.py
+++ b/solution.py
@@ -54,10 +54,18 @@
     return blk, chip * 2 + 1 - core, position, device
 
 
-def gather_kernel(
-    n, w_ref, hidden_ref, full_ref, pair_ref,
-    own_sem, own_send, own_recv, hid_send, hid_recv, ring_send, ring_recv, fwd_send, fwd_recv,
-):
+def gather_kernel(n, w_ref, hidden_ref, full_ref, pair_ref, hid_send, hid_recv, *sems):
+    def exchange(sibling):
+        return pltpu.make_async_remote_copy(
+            src_ref=hidden_ref, dst_ref=pair_ref, send_sem=hid_send, recv_sem=hid_recv,
+            device_id={"blk": sibling}, device_id_type=MESH,
+        )
+
+    gather_ring(n, w_ref, full_ref, sems, exchange, None)
+
+
+def gather_ring(n, w_ref, full_ref, sems, exchange, work):
+    own_sem, own_send, own_recv, ring_send, ring_recv, fwd_send, fwd_recv = sems
     blk, sibling, position, device = places(n)
     target = (device(position + 1), device(position - 1))
     quarter = w_ref.shape[0] // 4
@@ -102,13 +110,12 @@
         device_id={"blk": sibling}, device_id_type=MESH,
     )
     share.start()
-    share_hidden = pltpu.make_async_remote_copy(
-        src_ref=hidden_ref, dst_ref=pair_ref, send_sem=hid_send, recv_sem=hid_recv,
-        device_id={"blk": sibling}, device_id_type=MESH,
-    )
-    share_hidden.start()
+    if exchange is not None:
+        exchange(sibling).start()
 
     def step_body(step, carry):
+        if work is not None:
+            work(step - 1)
         for k in range(2):
             for way in range(2):
                 index = origin(way, step)
@@ -143,7 +150,28 @@
         src_ref=w_ref, dst_ref=full_ref.at[sibling], send_sem=own_send, recv_sem=own_recv,
         device_id={"blk": sibling}, device_id_type=MESH,
     ).wait_recv()
-    share_hidden.wait()
+    if exchange is not None:
+        exchange(sibling).wait()
+
+
+def gather_sems(n):
+    dma = pltpu.SemaphoreType.DMA
+    return [dma, dma, dma] + [dma((2, 2, n - 1))] * 4
+
+
+def scatter_scratch(n, tokens, height, width):
+    dma = pltpu.SemaphoreType.DMA
+    half = width // 2
+    return [
+        pltpu.VMEM((tokens, width), jnp.bfloat16),
+        pltpu.VMEM((2, height, half), jnp.float32),
+        pltpu.VMEM((2, n - 1, height, half), jnp.bfloat16),
+        pltpu.VMEM((2, n - 1, height, half), jnp.bfloat16),
+        dma,
+        dma,
+        dma((2, 2, n - 1)),
+        dma((2, 2, n - 1)),
+    ]
 
 
 def gather(w, hidden, blk_count):
@@ -158,7 +186,7 @@
         ),
         in_specs=[pl.BlockSpec(memory_space=pl.ANY)] * 2,
         out_specs=[pl.BlockSpec(memory_space=pl.ANY)] * 2,
-        scratch_shapes=[dma, dma, dma, dma, dma] + [dma((2, 2, n - 1))] * 4,
+        scratch_shapes=[dma, dma] + gather_sems(n),
         compiler_params=pltpu.CompilerParams(collective_id=0, has_side_effects=True),
         name="ring_gather",
     )(w, hidden)
@@ -166,34 +194,14 @@
 
 def scatter_kernel(
     n, tp_count, scale, hid_ref, mate_ref, grads_ref, term_ref, out_ref, recv_term_ref,
-    mate_grads, part, send_buf, recv_buf,
-    gr_send, gr_recv, term_send, term_recv, ring_send, ring_recv,
+    term_send, term_recv, *scratch,
 ):
-    blk, sibling, position, device = places(n)
-    target = (device(position + 1), device(position - 1))
+    chunk = term_ref.shape[1] // tp_count
     tp_me = lax.axis_index("tp")
-    height, width = out_ref.shape
-    half_rows, half = height // 2, width // 2
-    tile = 384 if half % 384 == 0 else 128
-    chunk = term_ref.shape[1] // tp_count
-    barrier = pltpu.get_barrier_semaphore()
-    for other in (sibling,) + target:
-        pl.semaphore_signal(barrier, inc=1, device_id={"blk": other}, device_id_type=MESH)
-    for k in range(1, tp_count):
-        pl.semaphore_signal(
-            barrier, inc=1, device_id={"tp": (tp_me + k) % tp_count}, device_id_type=MESH
-        )
-    pl.semaphore_wait(barrier, 3 + tp_count - 1)
-
-    share = pltpu.make_async_remote_copy(
-        src_ref=grads_ref, dst_ref=mate_grads, send_sem=gr_send, recv_sem=gr_recv,
-        device_id={"blk": sibling}, device_id_type=MESH,
-    )
-    share.start()
-    terms = []
-    for k in range(1, tp_count):
+
+    def copy(k):
         peer = (tp_me + k) % tp_count
-        copy = pltpu.make_async_remote_copy(
+        return pltpu.make_async_remote_copy(
             src_ref=term_ref.at[:, pl.ds(pl.multiple_of(peer * chunk, 128), chunk)],
             dst_ref=recv_term_ref.at[k - 1],
             send_sem=term_send.at[k - 1],
@@ -201,8 +209,42 @@
             device_id={"tp": peer},
             device_id_type=MESH,
         )
-        copy.start()
-        terms.append(copy)
+
+    def before():
+        for k in range(1, tp_count):
+            copy(k).start()
+
+    scatter_ring(
+        n, tp_count, scale, hid_ref, mate_ref, grads_ref, out_ref, scratch, before, None
+    )
+    for k in range(1, tp_count):
+        copy(k).wait()
+
+
+def scatter_ring(
+    n, tp_greet, scale, hid_ref, mate_ref, grads_ref, out_ref, scratch, before, work
+):
+    mate_grads, part, send_buf, recv_buf, gr_send, gr_recv, ring_send, ring_recv = scratch
+    blk, sibling, position, device = places(n)
+    target = (device(position + 1), device(position - 1))
+    height, width = out_ref.shape
+    half_rows, half = height // 2, width // 2
+    tile = 384 if half % 384 == 0 else 128
+    barrier = pltpu.get_barrier_semaphore()
+    for other in (sibling,) + target:
+        pl.semaphore_signal(barrier, inc=1, device_id={"blk": other}, device_id_type=MESH)
+    for k in range(1, tp_greet):
+        peer = (lax.axis_index("tp") + k) % tp_greet
+        pl.semaphore_signal(barrier, inc=1, device_id={"tp": peer}, device_id_type=MESH)
+    pl.semaphore_wait(barrier, 3 + tp_greet - 1)
+
+    share = pltpu.make_async_remote_copy(
+        src_ref=grads_ref, dst_ref=mate_grads, send_sem=gr_send, recv_sem=gr_recv,
+        device_id={"blk": sibling}, device_id_type=MESH,
+    )
+    share.start()
+    if before is not None:
+        before()
     share.wait()
 
     def ring_copy(way, k, step):
@@ -236,15 +278,16 @@
 
                 @pl.when(step > 0)
                 def _():
-                    before = step - 1
-                    ring_copy(way, k, before).wait_recv()
-                    part[way, spot] += recv_buf[way, before, spot].astype(jnp.float32)
+                    ring_copy(way, k, step - 1).wait_recv()
+                    part[way, spot] += recv_buf[way, step - 1, spot].astype(jnp.float32)
 
                 @pl.when(step < n - 1)
                 def _():
                     send_buf[way, step, spot] = part[way, spot].astype(jnp.bfloat16)
                     ring_copy(way, k, step).start()
 
+        if work is not None:
+            work(step)
         return carry
 
     lax.fori_loop(0, n, step_body, 0)
@@ -258,15 +301,12 @@
         return carry
 
     lax.fori_loop(0, n - 1, drain, 0)
-    for copy in terms:
-        copy.wait()
 
 
 def scatter(hidden, mate, grads, term, blk_count, tp_count, scale):
     n = blk_count // 2
     tokens, depth = hidden.shape
     height, width = depth // blk_count, grads.shape[1]
-    half = width // 2
     dma = pltpu.SemaphoreType.DMA
     vmem = pl.BlockSpec(memory_space=pltpu.VMEM)
     hbm = pl.BlockSpec(memory_space=pl.ANY)
@@ -278,18 +318,8 @@
         ),
         in_specs=[vmem, vmem, vmem, hbm],
         out_specs=[vmem, hbm],
-        scratch_shapes=[
-            pltpu.VMEM((tokens, width), jnp.bfloat16),
-            pltpu.VMEM((2, height, half), jnp.float32),
-            pltpu.VMEM((2, n - 1, height, half), jnp.bfloat16),
-            pltpu.VMEM((2, n - 1, height, half), jnp.bfloat16),
-            dma,
-            dma,
-            dma((tp_count - 1,)),
-            dma((tp_count - 1,)),
-            dma((2, 2, n - 1)),
-            dma((2, 2, n - 1)),
-        ],
+        scratch_shapes=[dma((tp_count - 1,)), dma((tp_count - 1,))]
+        + scatter_scratch(n, tokens, height, width),
         compiler_params=pltpu.CompilerParams(
             collective_id=1, has_side_effects=True, vmem_limit_bytes=VMEM_LIMIT
         ),
@@ -383,8 +413,259 @@
     )(starts, proj, proj, proj, key_cache, value_cache, grad_out)
 
 
+def head_work(heads, group, per_step, ins, outs, accs):
+    bias_ref, proj_ref, kc_ref, vc_ref, go_ref = ins
+    att_ref, grads_ref = outs
+    gk_acc, gv_acc = accs
+    kvs = heads // group
+    key_at, value_at = heads * HD, (heads + kvs) * HD
+    factor = HD ** (-0.5)
+    rows = proj_ref.shape[0]
+
+    def one(head):
+        g = head // group
+        q_cols = pl.ds(pl.multiple_of(head * HD, HD), HD)
+        kv_cols = pl.ds(pl.multiple_of(g * HD, HD), HD)
+        q, go = proj_ref[:, q_cols], go_ref[:, q_cols]
+        kn = proj_ref[:, pl.ds(pl.multiple_of(key_at + g * HD, HD), HD)]
+        vn = proj_ref[:, pl.ds(pl.multiple_of(value_at + g * HD, HD), HD)]
+        kc, vc = kc_ref[:, kv_cols], vc_ref[:, kv_cols]
+        s_c = contract_last(q, kc) + bias_ref[...]
+        row = lax.broadcasted_iota(jnp.int32, (rows, rows), 0)
+        col = lax.broadcasted_iota(jnp.int32, (rows, rows), 1)
+        s_o = jnp.where(col <= row, contract_last(q, kn), -jnp.inf)
+        top = jnp.maximum(
+            jnp.max(s_c, axis=-1, keepdims=True), jnp.max(s_o, axis=-1, keepdims=True)
+        )
+        e_c = jnp.exp2((s_c - top) * (factor * LOG2E))
+        e_o = jnp.exp2((s_o - top) * (factor * LOG2E))
+        total = jnp.sum(e_c, axis=-1, keepdims=True) + jnp.sum(e_o, axis=-1, keepdims=True)
+        inverse = 1.0 / total
+        p_c = (e_c * inverse).astype(jnp.bfloat16)
+        p_o = (e_o * inverse).astype(jnp.bfloat16)
+        att = jnp.dot(p_c, vc, preferred_element_type=jnp.float32) + jnp.dot(
+            p_o, vn, preferred_element_type=jnp.float32
+        )
+        att_ref[:, q_cols] = att.astype(jnp.bfloat16)
+        row_dot = jnp.sum(att * go.astype(jnp.float32), axis=-1, keepdims=True)
+        g_c = contract_last(go, vc) - row_dot
+        g_o = contract_last(go, vn) - row_dot
+        ds_c = (p_c.astype(jnp.float32) * g_c * factor).astype(jnp.bfloat16)
+        ds_o = (p_o.astype(jnp.float32) * g_o * factor).astype(jnp.bfloat16)
+        gq = jnp.dot(ds_c, kc, preferred_element_type=jnp.float32) + jnp.dot(
+            ds_o, kn, preferred_element_type=jnp.float32
+        )
+        grads_ref[:, q_cols] = gq.astype(jnp.bfloat16)
+        gk_acc[g] += contract_first(ds_o, q)
+        gv_acc[g] += contract_first(p_o, go)
+
+    def work(step):
+        def each(j, carry):
+            head = step * per_step + j
+
+            @pl.when(head < heads)
+            def _():
+                one(head)
+
+            return carry
+
+        lax.fori_loop(0, per_step, each, 0)
+
+    def finish():
+        for g in range(kvs):
+            grads_ref[:, key_at + g * HD : key_at + (g + 1) * HD] = gk_acc[g].astype(jnp.bfloat16)
+            grads_ref[:, value_at + g * HD : value_at + (g + 1) * HD] = gv_acc[g].astype(
+                jnp.bfloat16
+            )
+
+    gk_acc[...] = jnp.zeros_like(gk_acc)
+    gv_acc[...] = jnp.zeros_like(gv_acc)
+    return work, finish
+
+
+def gather_attend_kernel(
+    n, heads, group, w_ref, bias_ref, proj_ref, kc_ref, vc_ref, go_ref,
+    full_ref, att_ref, grads_ref, gk_acc, gv_acc, *sems,
+):
+    work, finish = head_work(
+        heads, group, -(-heads // (n - 1)), (bias_ref, proj_ref, kc_ref, vc_ref, go_ref),
+        (att_ref, grads_ref), (gk_acc, gv_acc),
+    )
+    gather_ring(n, w_ref, full_ref, sems, None, work)
+    finish()
+
+
+def scatter_attend_kernel(
+    n, heads, group, scale, hid_ref, mate_ref, done_ref, bias_ref, proj_ref, kc_ref, vc_ref,
+    go_ref, out_ref, att_ref, grads_ref, gk_acc, gv_acc, *scratch,
+):
+    work, finish = head_work(
+        heads, group, -(-heads // (n - 1)), (bias_ref, proj_ref, kc_ref, vc_ref, go_ref),
+        (att_ref, grads_ref), (gk_acc, gv_acc),
+    )
+    scatter_ring(n, 1, scale, hid_ref, mate_ref, done_ref, out_ref, scratch, None, work)
+    finish()
+
+
+def scatter_input_kernel(
+    n, scale, hid_ref, mate_ref, first_ref, second_ref, wa_ref, wb_ref, out_ref, gin_ref,
+    wa_buf, wb_buf, own, term, mate_term, wa_sem, wb_sem, term_send, term_recv, *scratch,
+):
+    tp_me = lax.axis_index("tp")
+    span = wa_buf.shape[1]
+    steps = n // 2
+
+    def load(c):
+        first_row = ((tp_me + 1 + c // steps) % 2) * (steps * span) + (c % steps) * span
+        at = pl.ds(pl.multiple_of(first_row, 128), span)
+        slot = c % 2
+        return (
+            pltpu.make_async_copy(wa_ref.at[at], wa_buf.at[slot], wa_sem.at[slot]),
+            pltpu.make_async_copy(wb_ref.at[at], wb_buf.at[slot], wb_sem.at[slot]),
+        )
+
+    def send():
+        return pltpu.make_async_remote_copy(
+            src_ref=term, dst_ref=mate_term, send_sem=term_send, recv_sem=term_recv,
+            device_id={"tp": (tp_me + 1) % 2}, device_id_type=MESH,
+        )
+
+    def before():
+        for copy in load(0):
+            copy.start()
+
+    def work(step):
+        @pl.when(step < n - 1)
+        def _():
+            for copy in load(step + 1):
+                copy.start()
+
+        for copy in load(step):
+            copy.wait()
+        value = contract_last(first_ref[...], wa_buf[step % 2]) + contract_last(
+            second_ref[...], wb_buf[step % 2]
+        )
+        at = pl.ds(pl.multiple_of((step % steps) * span, 128), span)
+
+        @pl.when(step < steps)
+        def _():
+            term[:, at] = value.astype(jnp.bfloat16)
+
+        @pl.when(step >= steps)
+        def _():
+            own[:, at] = value
+
+        @pl.when(step == steps - 1)
+        def _():
+            send().start()
+
+    scatter_ring(n, 2, scale, hid_ref, mate_ref, second_ref, out_ref, scratch, before, work)
+    send().wait()
+    gin_ref[...] = (own[...] + mate_term[...].astype(jnp.float32)).astype(jnp.bfloat16)
+
+
+def in_phases(blk_count, hidden, w_query, w_key, w_value, starts, key_cache, value_cache, grad_out):
+    n = blk_count // 2
+    tokens, depth = hidden.shape
+    height, cached, group = depth // blk_count, key_cache.shape[1], H // KV
+    kvs = w_key.shape[1] // HD // 2
+    heads = kvs * group
+    q_cols, kv_cols = heads * HD, kvs * HD
+    width = q_cols + 2 * kv_cols
+    scale = (tokens * blk_count) ** (-0.5)
+    f32, bf16 = jnp.float32, jnp.bfloat16
+    dma = pltpu.SemaphoreType.DMA
+    vmem = pl.BlockSpec(memory_space=pltpu.VMEM)
+    hbm = pl.BlockSpec(memory_space=pl.ANY)
+    shape = jax.ShapeDtypeStruct
+
+    def cut(i):
+        kv = slice(i * kv_cols, (i + 1) * kv_cols)
+        qs = slice(i * q_cols, (i + 1) * q_cols)
+        w = jnp.concatenate([w_query[:, qs], w_key[:, kv], w_value[:, kv]], 1)
+        return w, key_cache[0, :, kv], value_cache[0, :, kv], grad_out[:, qs]
+
+    def params(number):
+        return pltpu.CompilerParams(
+            collective_id=number, has_side_effects=True, vmem_limit_bytes=VMEM_LIMIT
+        )
+
+    def project(full):
+        return jnp.dot(hidden, full, preferred_element_type=f32).astype(bf16)
+
+    slots = lax.broadcasted_iota(jnp.int32, (1, cached), 1)
+    bias = jnp.where(slots < starts[0], 0.0, -jnp.inf).astype(f32)
+    accs = [pltpu.VMEM((kvs, tokens, HD), f32)] * 2
+    w_a, kc_a, vc_a, go_a = cut(0)
+    w_b, kc_b, vc_b, go_b = cut(1)
+    full_a, mate = gather(w_a, hidden, blk_count)
+    full_a = full_a.reshape(depth, width)
+    full_b, att_a, grads_a = pl.pallas_call(
+        functools.partial(gather_attend_kernel, n, heads, group),
+        out_shape=(
+            shape((blk_count, height, width), bf16),
+            shape((tokens, q_cols), bf16),
+            shape((tokens, width), bf16),
+        ),
+        in_specs=[hbm] + [vmem] * 5,
+        out_specs=[hbm, vmem, vmem],
+        scratch_shapes=accs + gather_sems(n),
+        compiler_params=params(1),
+        name="gather_attend",
+    )(w_b, bias, project(full_a), kc_a, vc_a, go_a)
+    full_b = full_b.reshape(depth, width)
+    sum_a, att_b, grads_b = pl.pallas_call(
+        functools.partial(scatter_attend_kernel, n, heads, group, scale),
+        out_shape=(
+            shape((height, width), f32),
+            shape((tokens, q_cols), bf16),
+            shape((tokens, width), bf16),
+        ),
+        in_specs=[vmem] * 8,
+        out_specs=[vmem] * 3,
+        scratch_shapes=accs + scatter_scratch(n, tokens, height, width),
+        compiler_params=params(2),
+        name="scatter_attend",
+    )(hidden, mate, grads_a, bias, project(full_b), kc_b, vc_b, go_b)
+    sum_b, grad_in = pl.pallas_call(
+        functools.partial(scatter_input_kernel, n, scale),
+        out_shape=(shape((height, width), f32), shape((tokens, depth // 2), bf16)),
+        in_specs=[vmem] * 4 + [hbm] * 2,
+        out_specs=[vmem] * 2,
+        scratch_shapes=[
+            pltpu.VMEM((2, depth // n, width), bf16),
+            pltpu.VMEM((2, depth // n, width), bf16),
+            pltpu.VMEM((tokens, depth // 2), f32),
+            pltpu.VMEM((tokens, depth // 2), bf16),
+            pltpu.VMEM((tokens, depth // 2), bf16),
+            dma((2,)),
+            dma((2,)),
+            dma,
+            dma,
+        ]
+        + scatter_scratch(n, tokens, height, width),
+        compiler_params=params(3),
+        name="scatter_input",
+    )(hidden, mate, grads_a, grads_b, full_a, full_b)
+
+    def join(first, last):
+        return jnp.concatenate([sum_a[:, first:last], sum_b[:, first:last]], 1)
+
+    return (
+        jnp.concatenate([att_a, att_b], 1),
+        grad_in,
+        join(0, q_cols),
+        join(q_cols, q_cols + kv_cols),
+        join(q_cols + kv_cols, width),
+    )
+
+
 def local(blk_count, tp_count, hidden_in, w_query, w_key, w_value, starts, key_cache, value_cache, grad_out):
     tokens_dev, depth = hidden_in.shape
+    if tp_count == 2 and (w_key.shape[1] // HD) % 2 == 0 and blk_count % 4 == 0:
+        return in_phases(
+            blk_count, hidden_in, w_query, w_key, w_value, starts, key_cache, value_cache, grad_out
+        )
     w = jnp.concatenate([w_query, w_key, w_value], 1)
     full, mate = gather(w, hidden_in, blk_count)
     full = full.reshape(depth, w.shape[1])

time: 355 us -> 322 us (0.907)
  Pallas kernels: 310 us -> 286 us
  matrix products: 33 us -> 18.3 us
  local copies, waits for them, and re-layouts: 4.29 us -> 9.76 us
    pallas_call x1, Pallas kernels: 127 us -> 67 us  [gather(): pl.pallas_call(functools.partial(gather_kernel, n), out_shape=(jax.ShapeD...]
    pallas_call x2 -> x3, Pallas kernels: 183 us -> 219 us  [the longest x1 76 us: in_phases(): pl.pallas_call(functools.partial(scatter_input_kernel, n, scale), out_sha...]
    dot_general x2, matrix products: 33 us -> 18.3 us  [project(): return jnp.dot(hidden, full, preferred_element_type=f32).astype(bf16)]
    convert_element_type x1 -> x0, other arithmetic: 4.18 us -> none  [local(): grad_in = grad_in.astype(jnp.bfloat16)]
where the time goes in v2:
time: 322 us; the launch traced here: 321 us
  Pallas kernels  286 us (89%)
  matrix products  18.3 us (6%)
  local copies, waits for them, and re-layouts  9.76 us (3%)
  other arithmetic  6.32 us (2%)
    pallas_call x1, Pallas kernels, in_phases(): pl.pallas_call(functools.partial(scatter_input_kernel, n, scale), out_sha...  76 us
    pallas_call x1, Pallas kernels, in_phases(): pl.pallas_call(functools.partial(scatter_attend_kernel, n, heads, group,...  73.2 us
    pallas_call x1, Pallas kernels, in_phases(): pl.pallas_call(functools.partial(gather_attend_kernel, n, heads, group),...  69.3 us
    pallas_call x1, Pallas kernels, gather(): pl.pallas_call(functools.partial(gather_kernel, n), out_shape=(jax.ShapeD...  67 us
    dot_general x2, matrix products, project(): return jnp.dot(hidden, full, preferred_element_type=f32).astype(bf16)  18.3 us

profile of v2, /device:TPU:0, one launch (start us, length us, event | category | flops | bytes accessed | tf_op | source)
XLA Modules:
  0.0 321.4 jit_solution(15578435653106526017)
XLA Ops:
  0.6 0.0 copy-start.7
  1.4 0.6 compare_select_fusion.bias_ref
  2.0 1.0 fusion.6
  3.0 1.0 fusion.7
  4.0 0.0 copy-done.7
  4.0 0.1 fusion.5
  4.0 0.0 copy-start.1
  4.1 1.2 pad_maximum_fusion.2
  5.3 0.7 copy-done.1
  6.0 1.3 fusion.4
  7.3 0.5 copy-done.5
  7.8 0.4 copy-done.6
  8.2 1.5 slice_bitcast_fusion
  9.7 67.0 %ring_gather.1 = (bf16[16,256,1536]{2,1,0:T(8,128)(2,1)}, bf16[384,4096]{1,0:T(8,128)(2,1)}) custom-call(bf16[256,1536]{1,0:T(8,128)(2,1)} %get-tuple-element.42.w_ref, bf16[384,4096]{1,0:T(8,128)(2,1)} %hid_ref.3), custom_call_target="tpu_custom_call" | custom-call | tf_op jit(solution)/shard_map/ring_gather/pallas_call | solution.py:181
  76.6 0.0 copy-done
  76.7 9.1 %fusion.proj_ref = bf16[384,1536]{1,0:T(8,128)(2,1)} fusion(bf16[384,4096]{1,0:T(8,128)(2,1)S(1)} %copy-done, bf16[4096,1536]{1,0:T(8,128)(2,1)} %bitcast.20), kind=kOutput, calls=%fused_computation.2 | convolution fusion | flops 4832428032 | bytes 16908288 | tf_op jit(solution)/shard_map/dot_general | solution.py:594
  85.8 69.3 %gather_attend.1 = (bf16[16,256,1536]{2,1,0:T(8,128)(2,1)}, bf16[384,1024]{1,0:T(8,128)(2,1)}, bf16[384,1536]{1,0:T(8,128)(2,1)}) custom-call(bf16[256,1536]{1,0:T(8,128)(2,1)} %get-tuple-element.41.w_ref, f32[1,1152]{1,0:T(1,128)} %compare_select_fusion.bias_ref, bf16[384,1536]{1,0:T(8,128)(2,1)} %fusion.proj_ref, ...), custom_call_target="tpu_custom_call" | custom-call | tf_op jit(solution)/shard_map/gather_attend/pallas_call | solution.py:603
  155.1 9.1 %fusion.1.proj_ref = bf16[384,1536]{1,0:T(8,128)(2,1)} fusion(bf16[384,4096]{1,0:T(8,128)(2,1)S(1)} %copy-done, bf16[4096,1536]{1,0:T(8,128)(2,1)} %bitcast.22), kind=kOutput, calls=%fused_computation.3 | convolution fusion | flops 4832428032 | bytes 16908288 | tf_op jit(solution)/shard_map/dot_general | solution.py:594
  164.3 73.2 %scatter_attend.1 = (f32[256,1536]{1,0:T(8,128)}, bf16[384,1024]{1,0:T(8,128)(2,1)}, bf16[384,1536]{1,0:T(8,128)(2,1)}) custom-call(bf16[384,4096]{1,0:T(8,128)(2,1)} %hid_ref.3, bf16[384,4096]{1,0:T(8,128)(2,1)} %get-tuple-element.17.mate_ref, bf16[384,1536]{1,0:T(8,128)(2,1)} %get-tuple-element.18.done_ref.first_ref, ...), custom_call_target="tpu_custom_call" | custom-call | tf_op jit(solution)/shard_map/scatter_attend/pallas_call | solution.py:617
  237.5 76.0 %scatter_input.1 = (f32[256,1536]{1,0:T(8,128)}, bf16[384,2048]{1,0:T(8,128)(2,1)}) custom-call(bf16[384,4096]{1,0:T(8,128)(2,1)} %hid_ref.3, bf16[384,4096]{1,0:T(8,128)(2,1)} %get-tuple-element.17.mate_ref, bf16[384,1536]{1,0:T(8,128)(2,1)} %get-tuple-element.18.done_ref.first_ref, bf16[384,1536]{1,0:T(8,128)(2,1)} %get-tuple-element.21.second_ref, ...), custom_call_target="tpu_custom_call" | custom-call | tf_op jit(solution)/shard_map/scatter_input/pallas_call | solution.py:630
  313.5 0.0 copy-done.8
  313.5 0.0 copy-done.9
  313.6 0.0 copy-start.4
  313.6 1.3 pad_maximum_fusion.1
  314.8 0.7 copy-done.4
  315.6 0.1 slice.67
  315.7 1.3 copy-done.3
  317.0 0.1 slice.66
  317.1 1.5 pad_maximum_fusion
  318.5 0.9 pad_maximum_fusion.5
  319.4 0.9 pad_maximum_fusion.4
  320.3 1.1 copy.19
  (10 shorter events, 0.1 us)
Async XLA Ops:
  0.6 3.3 %copy-start.7 = (bf16[256,2048]{1,0:T(8,128)(2,1)S(1)}, bf16[256,2048]{1,0:T(8,128)(2,1)}, u32[]{:S(2)}) copy-start(bf16[256,2048]{1,0:T(8,128)(2,1)} %param.9) | copy-start | bytes 3145732
  4.0 2.0 copy-start.1
  6.0 1.8 copy-start.5
  6.0 2.2 copy-start.6
  9.7 67.0 %copy-start = (bf16[384,4096]{1,0:T(8,128)(2,1)S(1)}, bf16[384,4096]{1,0:T(8,128)(2,1)}, u32[]{:S(2)}) copy-start(bf16[384,4096]{1,0:T(8,128)(2,1)} %hid_ref.3) | copy-start | bytes 9437188
  237.5 76.1 %copy-start.8 = (bf16[384,1024]{1,0:T(8,128)(2,1)S(1)}, bf16[384,1024]{1,0:T(8,128)(2,1)}, u32[]{:S(2)}) copy-start(bf16[384,1024]{1,0:T(8,128)(2,1)} %get-tuple-element.16) | copy-start | bytes 2359300
  237.5 76.1 %copy-start.9 = (bf16[384,1024]{1,0:T(8,128)(2,1)S(1)}, bf16[384,1024]{1,0:T(8,128)(2,1)}, u32[]{:S(2)}) copy-start(bf16[384,1024]{1,0:T(8,128)(2,1)} %get-tuple-element.20) | copy-start | bytes 2359300
  313.6 2.0 copy-start.4
  315.5 1.4 copy-start.3
  318.5 1.7 copy-start.2

commit v3 on v2

--- a/solution.py
+++ b/solution.py
@@ -413,8 +413,11 @@
     )(starts, proj, proj, proj, key_cache, value_cache, grad_out)
 
 
-def head_work(heads, group, per_step, ins, outs, accs):
-    bias_ref, proj_ref, kc_ref, vc_ref, go_ref = ins
+def head_work(heads, group, per_step, ins, outs, accs, hid_ref, full_ref, proj):
+    bias_ref, kc_ref, vc_ref, go_ref = ins
+    proj_ref, full_buf, full_sem = proj
+    load = pltpu.make_async_copy(full_ref, full_buf, full_sem)
+    load.start()
     att_ref, grads_ref = outs
     gk_acc, gv_acc = accs
     kvs = heads // group
@@ -459,17 +462,37 @@
         gk_acc[g] += contract_first(ds_o, q)
         gv_acc[g] += contract_first(p_o, go)
 
+    def project():
+        load.wait()
+        width = proj_ref.shape[1]
+        tile = 384 if width % 384 == 0 else 128
+
+        def each(t, carry):
+            at = pl.ds(pl.multiple_of(t * tile, 128), tile)
+            proj_ref[:, at] = jnp.dot(
+                hid_ref[...], full_buf[:, at], preferred_element_type=jnp.float32
+            ).astype(jnp.bfloat16)
+            return carry
+
+        lax.fori_loop(0, width // tile, each, 0)
+
     def work(step):
-        def each(j, carry):
-            head = step * per_step + j
-
-            @pl.when(head < heads)
-            def _():
-                one(head)
-
-            return carry
-
-        lax.fori_loop(0, per_step, each, 0)
+        @pl.when(step == 0)
+        def _():
+            project()
+
+        @pl.when(step > 0)
+        def _():
+            def each(j, carry):
+                head = (step - 1) * per_step + j
+
+                @pl.when(head < heads)
+                def _():
+                    one(head)
+
+                return carry
+
+            lax.fori_loop(0, per_step, each, 0)
 
     def finish():
         for g in range(kvs):
@@ -484,24 +507,24 @@
 
 
 def gather_attend_kernel(
-    n, heads, group, w_ref, bias_ref, proj_ref, kc_ref, vc_ref, go_ref,
-    full_ref, att_ref, grads_ref, gk_acc, gv_acc, *sems,
+    n, heads, group, w_ref, prev_ref, hid_ref, bias_ref, kc_ref, vc_ref, go_ref,
+    full_ref, att_ref, grads_ref, gk_acc, gv_acc, proj, full_buf, full_sem, *sems,
 ):
     work, finish = head_work(
-        heads, group, -(-heads // (n - 1)), (bias_ref, proj_ref, kc_ref, vc_ref, go_ref),
-        (att_ref, grads_ref), (gk_acc, gv_acc),
+        heads, group, -(-heads // (n - 2)), (bias_ref, kc_ref, vc_ref, go_ref),
+        (att_ref, grads_ref), (gk_acc, gv_acc), hid_ref, prev_ref, (proj, full_buf, full_sem),
     )
     gather_ring(n, w_ref, full_ref, sems, None, work)
     finish()
 
 
 def scatter_attend_kernel(
-    n, heads, group, scale, hid_ref, mate_ref, done_ref, bias_ref, proj_ref, kc_ref, vc_ref,
-    go_ref, out_ref, att_ref, grads_ref, gk_acc, gv_acc, *scratch,
+    n, heads, group, scale, hid_ref, mate_ref, done_ref, full_ref, bias_ref, kc_ref, vc_ref,
+    go_ref, out_ref, att_ref, grads_ref, gk_acc, gv_acc, proj, full_buf, full_sem, *scratch,
 ):
     work, finish = head_work(
-        heads, group, -(-heads // (n - 1)), (bias_ref, proj_ref, kc_ref, vc_ref, go_ref),
-        (att_ref, grads_ref), (gk_acc, gv_acc),
+        heads, group, -(-heads // (n - 2)), (bias_ref, kc_ref, vc_ref, go_ref),
+        (att_ref, grads_ref), (gk_acc, gv_acc), hid_ref, full_ref, (proj, full_buf, full_sem),
     )
     scatter_ring(n, 1, scale, hid_ref, mate_ref, done_ref, out_ref, scratch, None, work)
     finish()
@@ -590,12 +613,10 @@
             collective_id=number, has_side_effects=True, vmem_limit_bytes=VMEM_LIMIT
         )
 
-    def project(full):
-        return jnp.dot(hidden, full, preferred_element_type=f32).astype(bf16)
-
     slots = lax.broadcasted_iota(jnp.int32, (1, cached), 1)
     bias = jnp.where(slots < starts[0], 0.0, -jnp.inf).astype(f32)
     accs = [pltpu.VMEM((kvs, tokens, HD), f32)] * 2
+    accs += [pltpu.VMEM((tokens, width), bf16), pltpu.VMEM((depth, width), bf16), dma]
     w_a, kc_a, vc_a, go_a = cut(0)
     w_b, kc_b, vc_b, go_b = cut(1)
     full_a, mate = gather(w_a, hidden, blk_count)
@@ -607,12 +628,12 @@
             shape((tokens, q_cols), bf16),
             shape((tokens, width), bf16),
         ),
-        in_specs=[hbm] + [vmem] * 5,
+        in_specs=[hbm] * 2 + [vmem] * 5,
         out_specs=[hbm, vmem, vmem],
         scratch_shapes=accs + gather_sems(n),
         compiler_params=params(1),
         name="gather_attend",
-    )(w_b, bias, project(full_a), kc_a, vc_a, go_a)
+    )(w_b, full_a, hidden, bias, kc_a, vc_a, go_a)
     full_b = full_b.reshape(depth, width)
     sum_a, att_b, grads_b = pl.pallas_call(
         functools.partial(scatter_attend_kernel, n, heads, group, scale),
@@ -621,12 +642,12 @@
             shape((tokens, q_cols), bf16),
             shape((tokens, width), bf16),
         ),
-        in_specs=[vmem] * 8,
+        in_specs=[vmem] * 3 + [hbm] + [vmem] * 4,
         out_specs=[vmem] * 3,
         scratch_shapes=accs + scatter_scratch(n, tokens, height, width),
         compiler_params=params(2),
         name="scatter_attend",
-    )(hidden, mate, grads_a, bias, project(full_b), kc_b, vc_b, go_b)
+    )(hidden, mate, grads_a, full_b, bias, kc_b, vc_b, go_b)
     sum_b, grad_in = pl.pallas_call(
         functools.partial(scatter_input_kernel, n, scale),
         out_shape=(shape((height, width), f32), shape((tokens, depth // 2), bf16)),

time: 322 us -> 307 us (0.953)
  matrix products: 18.3 us -> 0 us
    dot_general x2 -> x0, matrix products: 18.3 us -> none  [project(): return jnp.dot(hidden, full, preferred_element_type=f32).astype(bf16)]
where the time goes in v3:
time: 307 us
  Pallas kernels  289 us (94%)
  local copies, waits for them, and re-layouts  9.78 us (3%)
  other arithmetic  6.32 us (2%)
    pallas_call x1, Pallas kernels, in_phases(): pl.pallas_call(functools.partial(scatter_input_kernel, n, scale), out_sha...  76.1 us
    pallas_call x1, Pallas kernels, in_phases(): pl.pallas_call(functools.partial(scatter_attend_kernel, n, heads, group,...  74.1 us
    pallas_call x1, Pallas kernels, in_phases(): pl.pallas_call(functools.partial(gather_attend_kernel, n, heads, group),...  72 us
    pallas_call x1, Pallas kernels, gather(): pl.pallas_call(functools.partial(gather_kernel, n), out_shape=(jax.ShapeD...  67 us

profile of v3, /device:TPU:0, one launch (start us, length us, event | category | flops | bytes accessed | tf_op | source)
XLA Modules:
  0.0 306.8 jit_solution(7890113537108795336)
XLA Ops:
  0.6 0.0 copy-start.6
  1.4 0.6 compare_select_fusion.bias_ref
  2.0 1.0 fusion.4
  3.0 1.0 fusion.5
  4.0 0.0 copy-done.6
  4.0 0.1 fusion.3
  4.0 0.0 copy-start
  4.1 1.2 pad_maximum_fusion.2
  5.3 0.7 copy-done
  6.0 1.3 fusion.2
  7.3 0.5 copy-done.4
  7.8 0.4 copy-done.5
  8.2 1.5 slice_bitcast_fusion
  9.7 67.0 %ring_gather.1 = (bf16[16,256,1536]{2,1,0:T(8,128)(2,1)}, bf16[384,4096]{1,0:T(8,128)(2,1)}) custom-call(bf16[256,1536]{1,0:T(8,128)(2,1)} %get-tuple-element.42.w_ref, bf16[384,4096]{1,0:T(8,128)(2,1)} %hid_ref.5), custom_call_target="tpu_custom_call" | custom-call | tf_op jit(solution)/shard_map/ring_gather/pallas_call | solution.py:181
  76.7 72.0 %gather_attend.1 = (bf16[16,256,1536]{2,1,0:T(8,128)(2,1)}, bf16[384,1024]{1,0:T(8,128)(2,1)}, bf16[384,1536]{1,0:T(8,128)(2,1)}) custom-call(bf16[256,1536]{1,0:T(8,128)(2,1)} %get-tuple-element.41.w_ref, bf16[4096,1536]{1,0:T(8,128)(2,1)} %bitcast.12, bf16[384,4096]{1,0:T(8,128)(2,1)} %hid_ref.5, f32[1,1152]{1,0:T(1,128)} %compare_select_fusion.bias_ref, ...), custom_call_target="tpu_custom_call" | custom-call | tf_op jit(solution)/shard_map/gather_attend/pallas_call | solution.py:624
  148.6 74.1 %scatter_attend.1 = (f32[256,1536]{1,0:T(8,128)}, bf16[384,1024]{1,0:T(8,128)(2,1)}, bf16[384,1536]{1,0:T(8,128)(2,1)}) custom-call(bf16[384,4096]{1,0:T(8,128)(2,1)} %hid_ref.5, bf16[384,4096]{1,0:T(8,128)(2,1)} %get-tuple-element.17.mate_ref, bf16[384,1536]{1,0:T(8,128)(2,1)} %get-tuple-element.18.done_ref.first_ref, bf16[4096,1536]{1,0:T(8,128)(2,1)} %bitcast.14, ...), custom_call_target="tpu_custom_call" | custom-call | tf_op jit(solution)/shard_map/scatter_attend/pallas_call | solution.py:638
  222.8 0.0 copy-start.7
  222.8 0.0 copy-start.8
  222.8 76.1 %scatter_input.1 = (f32[256,1536]{1,0:T(8,128)}, bf16[384,2048]{1,0:T(8,128)(2,1)}) custom-call(bf16[384,4096]{1,0:T(8,128)(2,1)} %hid_ref.5, bf16[384,4096]{1,0:T(8,128)(2,1)} %get-tuple-element.17.mate_ref, bf16[384,1536]{1,0:T(8,128)(2,1)} %get-tuple-element.18.done_ref.first_ref, bf16[384,1536]{1,0:T(8,128)(2,1)} %get-tuple-element.21.second_ref, ...), custom_call_target="tpu_custom_call" | custom-call | tf_op jit(solution)/shard_map/scatter_input/pallas_call | solution.py:651
  298.9 0.0 copy-done.7
  298.9 0.0 copy-done.8
  298.9 0.0 copy-start.3
  298.9 1.3 pad_maximum_fusion.1
  300.2 0.7 copy-done.3
  300.9 0.1 slice.67
  301.0 1.3 copy-done.2
  302.3 0.1 slice.66
  302.4 1.5 pad_maximum_fusion
  303.9 0.9 pad_maximum_fusion.5
  304.8 0.9 pad_maximum_fusion.4
  305.6 0.0 copy-done.1
  305.6 1.1 copy.15
  (6 shorter events, 0.1 us)
Async XLA Ops:
  0.6 3.3 %copy-start.6 = (bf16[256,2048]{1,0:T(8,128)(2,1)S(1)}, bf16[256,2048]{1,0:T(8,128)(2,1)}, u32[]{:S(2)}) copy-start(bf16[256,2048]{1,0:T(8,128)(2,1)} %param.9) | copy-start | bytes 3145732
  4.0 2.0 copy-start
  6.0 1.8 copy-start.4
  6.0 2.2 copy-start.5
  222.8 76.1 %copy-start.7 = (bf16[384,1024]{1,0:T(8,128)(2,1)S(1)}, bf16[384,1024]{1,0:T(8,128)(2,1)}, u32[]{:S(2)}) copy-start(bf16[384,1024]{1,0:T(8,128)(2,1)} %get-tuple-element.16) | copy-start | bytes 2359300
  222.8 76.1 %copy-start.8 = (bf16[384,1024]{1,0:T(8,128)(2,1)S(1)}, bf16[384,1024]{1,0:T(8,128)(2,1)}, u32[]{:S(2)}) copy-start(bf16[384,1024]{1,0:T(8,128)(2,1)} %get-tuple-element.20) | copy-start | bytes 2359300
  298.9 2.0 copy-start.3
  300.9 1.4 copy-start.2
  303.9 1.7 copy-start.1
